TPU v7x, 32 devices: a whole 2x2x4 slice. The times are simulated.
32 devices in a mesh: grp: 2 (over x), dp: 4 (over z), tp: 4 (over y, core).
Axes of the slice: x: 2, y: 2, z: 4, core: 2. Of those that a mesh axis runs over, the one named last changes fastest.
Arguments:
- tokens: bfloat16 [16384, 768], P(('grp', 'dp', 'tp')), may hold values from -6 to 6
- patch_side: int32 [8], P(('grp', 'dp')), may hold values from 8 to 48, as said below
- gain_attn: float32 [768], replicated, may hold values from 0.25 to 1.75
- w_qkv: bfloat16 [768, 2304], P(None, 'tp'), may hold values from -0.21875 to 0.21875
- w_out: bfloat16 [768, 768], P('tp'), may hold values from -0.875 to 0.875
- gain_mlp: float32 [768], replicated, may hold values from 0.25 to 1.75
- w_up: bfloat16 [768, 3072], P(None, 'tp'), may hold values from -0.21875 to 0.21875
- w_down: bfloat16 [3072, 768], P('tp'), may hold values from -0.109375 to 0.109375
- cotangent: bfloat16 [16384, 768], P(('grp', 'dp', 'tp')), may hold values from -6 to 6
Outputs:
- mixed_rows: bfloat16 [16384, 768], P(('grp', 'dp', 'tp'))
- input_grad: float32 [16384, 768], P(('grp', 'dp', 'tp'))
- grad_gain_attn: float32 [768], replicated
- grad_qkv: float32 [768, 2304], P('dp', 'tp')
- grad_out: float32 [768, 768], P('tp', 'dp')
- grad_gain_mlp: float32 [768], replicated
- grad_up: float32 [768, 3072], P('dp', 'tp')
- grad_down: float32 [3072, 768], P('tp', 'dp')
Inputs may be any that keep to these rules, and one draw needn't show every extreme that they name: `patch_side`: every entry is one of 8, 10, 12, 16, 20, 24, 30, 40, 48; some group has 8 and some 48.
All inputs are finite; a program needn't handle non-finite values.
Results may differ from a plain program's by a relative error of at most 0.012.
The roundings to bfloat16 on the way count: a program that leaves them out, or rounds other values in their place, can miss the bound.
Values may be sent and summed in bfloat16 or wider, within the bound.
No kernel may reach another device: no remote copies, remote signals or barrier semaphores. Data moves between devices by JAX's collectives and lax.ppermute only.
A program may use at most 128 MiB of HBM per device.

v0:
```python
from functools import partial

import jax
import jax.numpy as jnp
from jax import lax
from jax.sharding import PartitionSpec as P

HD = 64
IMAGE = 240


epsilon = 1e-06


def segments(patch_size, length):
    cell_count = (IMAGE // patch_size) ** 2
    positions = jnp.arange(length, dtype=jnp.int32)
    return jnp.minimum(positions // cell_count, length // cell_count).astype(jnp.int32)


def normalize(values, scaling):
    centred = values - jnp.mean(values, axis=1, keepdims=True)
    inverse = lax.rsqrt(jnp.mean(centred * centred, axis=1, keepdims=True) + epsilon)
    normed = centred * inverse
    return (normed * scaling, normed, inverse)


def restore(d_normed, normed, inverse, scaling):
    d_scaled = d_normed * scaling
    return inverse * (
        d_scaled
        - jnp.mean(d_scaled, axis=1, keepdims=True)
        - normed * jnp.mean(d_scaled * normed, axis=1, keepdims=True)
    )


def masked_scores(q_rows, key_rows, query_ids, image_id):
    scores = (
        jnp.einsum("qhd,khd->hqk", q_rows, key_rows, preferred_element_type=jnp.float32) * 0.125
    )
    return jnp.where(query_ids[None, :, None] == image_id[None, None, :], scores, -1e30)


def attend(queries, key_rows, values, image_id):
    length = queries.shape[0]
    block_rows = min(512, length)

    def block_out(number):
        first_row = number * block_rows
        q_rows = lax.dynamic_slice_in_dim(queries, first_row, block_rows, 0)
        query_ids = lax.dynamic_slice_in_dim(image_id, first_row, block_rows, 0)
        scores = masked_scores(q_rows, key_rows, query_ids, image_id)
        largest = jnp.max(scores, axis=2, keepdims=True)
        exponent = jnp.exp(scores - largest)
        total = jnp.sum(exponent, axis=2, keepdims=True)
        attn_probs = (exponent / total).astype(jnp.bfloat16)
        heads_out = jnp.einsum(
            "hqk,khd->qhd", attn_probs, values, preferred_element_type=jnp.float32
        )
        return (heads_out.astype(jnp.bfloat16), (largest + jnp.log(total))[:, :, 0])

    heads_out, log_total = lax.map(block_out, jnp.arange(length // block_rows, dtype=jnp.int32))
    return (heads_out.reshape(length, -1), log_total)


def attend_back(queries, key_rows, values, image_id, log_total, d_heads):
    length, head_count, width = queries.shape
    block_rows = min(512, length)

    def block_back(carry, number):
        d_keys, d_values = carry
        first_row = number * block_rows
        q_rows = lax.dynamic_slice_in_dim(queries, first_row, block_rows, 0)
        query_ids = lax.dynamic_slice_in_dim(image_id, first_row, block_rows, 0)
        d_rows = lax.dynamic_slice_in_dim(d_heads, first_row, block_rows, 0)
        scores = masked_scores(q_rows, key_rows, query_ids, image_id)
        attn_probs = jnp.exp(scores - log_total[number][:, :, None])
        d_values = d_values + jnp.einsum(
            "hqk,qhd->khd",
            attn_probs.astype(jnp.bfloat16),
            d_rows,
            preferred_element_type=jnp.float32,
        )
        d_probs = jnp.einsum("qhd,khd->hqk", d_rows, values, preferred_element_type=jnp.float32)
        d_scores = attn_probs * (d_probs - jnp.sum(attn_probs * d_probs, axis=2, keepdims=True))
        d_scores = d_scores.astype(jnp.bfloat16)
        d_query = (
            jnp.einsum("hqk,khd->qhd", d_scores, key_rows, preferred_element_type=jnp.float32)
            * 0.125
        )
        d_keys = (
            d_keys
            + jnp.einsum("hqk,qhd->khd", d_scores, q_rows, preferred_element_type=jnp.float32)
            * 0.125
        )
        return ((d_keys, d_values), d_query.astype(jnp.bfloat16))

    zero_rows = jnp.zeros((length, head_count, width), jnp.float32)
    (d_keys, d_values), d_query = lax.scan(
        block_back, (zero_rows, zero_rows), jnp.arange(length // block_rows, dtype=jnp.int32)
    )
    d_query = d_query.reshape(length, head_count, width)
    stacked = jnp.stack(
        [d_query, d_keys.astype(jnp.bfloat16), d_values.astype(jnp.bfloat16)], axis=2
    )
    return stacked.reshape(length, -1)


def on_device(tokens, patch_side, gain_attn, w_qkv, w_out, gain_mlp, w_up, w_down, cotangent):
    activations = tokens.astype(jnp.float32)
    normed_attn, unit_attn, inverse_attn = normalize(activations, gain_attn)
    attn_in = lax.all_gather(normed_attn.astype(jnp.bfloat16), "tp", axis=0, tiled=True)
    group_rows = attn_in.shape[0]
    image_id = segments(patch_side[0], group_rows)
    head_count = w_out.shape[0] // HD
    qkv = jnp.dot(attn_in, w_qkv, preferred_element_type=jnp.float32).astype(jnp.bfloat16)
    qkv = qkv.reshape(group_rows, head_count, 3, HD)
    queries = qkv[:, :, 0]
    key_rows = qkv[:, :, 1]
    values = qkv[:, :, 2]
    heads_out, log_total = attend(queries, key_rows, values, image_id)
    picked = heads_out
    resid = activations + lax.psum_scatter(
        jnp.dot(picked, w_out, preferred_element_type=jnp.float32),
        "tp",
        scatter_dimension=0,
        tiled=True,
    )
    normed_mlp, unit_mlp, inverse_mlp = normalize(resid, gain_mlp)
    mlp_in = lax.all_gather(normed_mlp.astype(jnp.bfloat16), "tp", axis=0, tiled=True)
    pre_act = jnp.dot(mlp_in, w_up, preferred_element_type=jnp.float32)
    act = jax.nn.gelu(pre_act, approximate=False).astype(jnp.bfloat16)
    picked = act
    mixed_rows = (
        resid
        + lax.psum_scatter(
            jnp.dot(picked, w_down, preferred_element_type=jnp.float32).astype(jnp.bfloat16),
            "tp",
            scatter_dimension=0,
            tiled=True,
        ).astype(jnp.float32)
    ).astype(jnp.bfloat16)
    out_grads = lax.all_gather(cotangent, "tp", axis=0, tiled=True)
    grad_down = jnp.einsum("tf,td->fd", act, out_grads, preferred_element_type=jnp.float32)
    d_act = jnp.einsum("td,fd->tf", out_grads, w_down, preferred_element_type=jnp.float32)
    gelu_pull = jax.vjp(partial(jax.nn.gelu, approximate=False), pre_act)[1]
    d_pre = gelu_pull(d_act)[0].astype(jnp.bfloat16)
    grad_up = jnp.einsum("td,tf->df", mlp_in, d_pre, preferred_element_type=jnp.float32)
    picked = d_pre
    d_mlp_in = lax.psum_scatter(
        jnp.einsum("tf,df->td", picked, w_up, preferred_element_type=jnp.float32),
        "tp",
        scatter_dimension=0,
        tiled=True,
    )
    d_resid = cotangent.astype(jnp.float32) + restore(d_mlp_in, unit_mlp, inverse_mlp, gain_mlp)
    gain_part_mlp = jnp.sum(d_mlp_in * unit_mlp, axis=0)
    branch_grads = lax.all_gather(d_resid.astype(jnp.bfloat16), "tp", axis=0, tiled=True)
    grad_out = jnp.einsum("tk,td->kd", heads_out, branch_grads, preferred_element_type=jnp.float32)
    d_heads = jnp.einsum("td,kd->tk", branch_grads, w_out, preferred_element_type=jnp.float32)
    d_heads = d_heads.astype(jnp.bfloat16).reshape(group_rows, head_count, HD)
    d_qkv = attend_back(queries, key_rows, values, image_id, log_total, d_heads)
    grad_qkv = jnp.einsum("td,tc->dc", attn_in, d_qkv, preferred_element_type=jnp.float32)
    picked = d_qkv
    d_attn_in = lax.psum_scatter(
        jnp.einsum("tc,dc->td", picked, w_qkv, preferred_element_type=jnp.float32),
        "tp",
        scatter_dimension=0,
        tiled=True,
    )
    input_grad = d_resid + restore(d_attn_in, unit_attn, inverse_attn, gain_attn)
    gain_part_attn = jnp.sum(d_attn_in * unit_attn, axis=0)
    shard_qkv, shard_out, shard_up, shard_down = (
        lax.psum_scatter(grad_qkv, "dp", scatter_dimension=0, tiled=True),
        lax.psum_scatter(grad_out, "dp", scatter_dimension=1, tiled=True),
        lax.psum_scatter(grad_up, "dp", scatter_dimension=0, tiled=True),
        lax.psum_scatter(grad_down, "dp", scatter_dimension=1, tiled=True),
    )
    gain_attn_sum, gain_mlp_sum = lax.psum((gain_part_attn, gain_part_mlp), ("dp", "tp"))
    totals = lax.psum(
        (shard_qkv, shard_out, shard_up, shard_down, gain_attn_sum, gain_mlp_sum), "grp"
    )
    return (
        mixed_rows,
        input_grad,
        totals[4],
        totals[0],
        totals[1],
        totals[5],
        totals[2],
        totals[3],
    )


def solution(mesh):
    in_specs = (
        P(("grp", "dp", "tp"), None),
        P(("grp", "dp")),
        P(),
        P(None, "tp"),
        P("tp", None),
        P(),
        P(None, "tp"),
        P("tp", None),
        P(("grp", "dp", "tp"), None),
    )
    out_specs = (
        P(("grp", "dp", "tp"), None),
        P(("grp", "dp", "tp"), None),
        P(),
        P("dp", "tp"),
        P("tp", "dp"),
        P(),
        P("dp", "tp"),
        P("tp", "dp"),
    )
    return jax.shard_map(
        on_device, mesh=mesh, in_specs=in_specs, out_specs=out_specs, check_vma=False
    )
```

profile of v0, /device:TPU:0, one launch (start us, length us, event | category | flops | bytes accessed | tf_op | source)
XLA Modules:
  0.0 778.5 jit_solution(10367581245888826991)
XLA Ops:
  14.0 30.5 %all-gather.5.cloned.1.call-done = bf16[2048,768]{1,0:T(8,128)(2,1)} async-done(((bf16[512,768]{1,0:T(8,128)(2,1)}), bf16[2048,768]{1,0:T(8,128)(2,1)}) %all-gather.5.cloned.1.call-update) | async-done | bytes 3145744 | tf_op jit(solution)/shard_map/all_gather | solution.py:112
  49.6 90.6 %while.27 = (s32[]{:T(128)}, bf16[4,512,3,64]{1,3,2,0:T(8,128)(2,1)}, f32[4,3,512]{2,1,0:T(4,128)}, s32[4]{0:T(128)S(1)}, s32[2048]{0:T(1024)S(1)}, /*index=5*/b...) while((s32[]{:T(128)}, ...), condition=%wide.region_5.6_spmd, body=%wide.region_2.5_spmd.sunk | while | flops 844200448 | bytes 43974852 | solution.py:62
  51.6 6.0 fusion.120
  57.6 6.8 fusion.121
  64.3 7.3 fusion.122
  74.2 6.0 fusion.120
  80.2 6.8 fusion.121
  87.0 7.3 fusion.122
  96.9 6.0 fusion.120
  102.9 6.8 fusion.121
  109.6 7.3 fusion.122
  119.5 6.0 fusion.120
  125.5 6.8 fusion.121
  132.3 7.3 fusion.122
  147.2 58.5 %reduce-scatter.11.cloned.1.call-done = f32[512,768]{1,0:T(8,128)} async-done(((f32[2048,768]{1,0:T(8,128)}), f32[512,768]{1,0:T(8,128)}) %reduce-scatter.11.cloned.1.call-update) | async-done | bytes 1572880 | tf_op jit(solution)/shard_map/reduce_scatter | solution.py:123
  210.7 27.6 %all-gather.7.cloned.1.call-done = bf16[2048,768]{1,0:T(8,128)(2,1)} async-done(((bf16[512,768]{1,0:T(8,128)(2,1)}), bf16[2048,768]{1,0:T(8,128)(2,1)}) %all-gather.7.cloned.1.call-update) | async-done | bytes 3145744 | tf_op jit(solution)/shard_map/all_gather | solution.py:130
  238.3 7.5 fusion.63
  245.7 22.6 %all-gather.9.cloned.1.call-done = bf16[2048,768]{1,0:T(8,128)(2,1)} async-done(((bf16[512,768]{1,0:T(8,128)(2,1)}), bf16[2048,768]{1,0:T(8,128)(2,1)}) %all-gather.9.cloned.1.call-update) | async-done | bytes 3145744 | tf_op jit(solution)/shard_map/all_gather | solution.py:143
  268.3 19.2 %add_convert_fusion = (bf16[2048,768]{1,0:T(8,128)(2,1)S(1)}, f32[2048,768]{1,0:T(8,128)}) fusion(f32[2048,768]{1,0:T(8,128)} %fusion.63, bf16[2048,768]{1,0:T(8,128)(2,1)} %all-gather.9.cloned.1.call-done, bf16[768,768]{1,0:T(8,128)(2,1)S(1)} %copy-done), kind=kOutput, calls=%fused_computation.47 | convolution fusion | flops 2529165312 | bytes 20054016 | tf_op jit(solution)/shard_map/td,fd->tf/dot_general | solution.py:145
  293.8 5.5 multiply_convert_fusion.1
  305.1 47.2 %reduce-scatter.15.cloned.1.call-done = f32[512,768]{1,0:T(8,128)} async-done(((f32[2048,768]{1,0:T(8,128)}), f32[512,768]{1,0:T(8,128)}) %reduce-scatter.15.cloned.1.call-update) | async-done | bytes 1572880 | tf_op jit(solution)/shard_map/reduce_scatter | solution.py:150
  355.5 37.2 %reduce-scatter.13.cloned.1.call-done = bf16[512,768]{1,0:T(8,128)(2,1)} async-done(((bf16[2048,768]{1,0:T(8,128)(2,1)}), bf16[512,768]{1,0:T(8,128)(2,1)}) %reduce-scatter.13.cloned.1.call-update) | async-done | bytes 786448 | tf_op jit(solution)/shard_map/reduce_scatter | solution.py:136
  397.5 28.5 %all-gather.11.cloned.1.call-done = bf16[2048,768]{1,0:T(8,128)(2,1)} async-done(((bf16[512,768]{1,0:T(8,128)(2,1)}), bf16[2048,768]{1,0:T(8,128)(2,1)}) %all-gather.11.cloned.1.call-update) | async-done | bytes 3145744 | tf_op jit(solution)/shard_map/all_gather | solution.py:158
  430.2 6.9 fusion.68
  437.2 7.0 fusion.67
  448.3 142.4 %while.28 = (s32[]{:T(128)}, f32[2048,3,64]{0,2,1:T(8,128)}, f32[2048,3,64]{0,2,1:T(8,128)}, bf16[4,512,3,64]{1,3,2,0:T(8,128)(2,1)}, s32[4]{0:T(128)S(1)}, /*in...) while((s32[]{:T(128)}, f32[2048,3,64]{0,2,1:T(8,128)}, ...), condition=%wide.region_15.16_spmd.clone, body=%wide.region_13.15_spmd.clone.sunk | while | flops 2063661568 | bytes 156494352 | solution.py:99
  456.3 4.7 fusion.134
  461.0 5.9 multiply_reduce_fusion.7
  466.9 6.1 multiply_convert_fusion.4
  473.0 5.9 fusion.135
  490.4 6.1 fusion.134
  496.5 5.8 multiply_reduce_fusion.7
  502.3 6.1 multiply_convert_fusion.4
  508.4 6.2 fusion.135
  526.6 6.1 fusion.134
  532.7 5.8 multiply_reduce_fusion.7
  538.5 6.1 multiply_convert_fusion.4
  544.6 5.9 fusion.135
  562.5 6.1 fusion.134
  568.6 5.8 multiply_reduce_fusion.7
  574.3 6.1 multiply_convert_fusion.4
  580.5 5.8 fusion.135
  601.1 4.6 fusion.65
  607.6 35.0 %reduce-scatter.19.cloned.1.call-done = f32[192,576]{1,0:T(8,128)} async-done(((f32[768,576]{1,0:T(8,128)}), f32[192,576]{1,0:T(8,128)}) %reduce-scatter.19.cloned.1.call-update) | async-done | bytes 442384 | tf_op jit(solution)/shard_map/reduce_scatter | solution.py:174
  642.6 60.2 %reduce-scatter.17.cloned.1.call-done = f32[512,768]{1,0:T(8,128)} async-done(((f32[2048,768]{1,0:T(8,128)}), f32[512,768]{1,0:T(8,128)}) %reduce-scatter.17.cloned.1.call-update) | async-done | bytes 1572880 | tf_op jit(solution)/shard_map/reduce_scatter | solution.py:165
  705.0 32.7 %all-reduce = (f32[768]{0:T(1024)S(1)}, f32[768]{0:T(1024)S(1)}) all-reduce(f32[768]{0:T(1024)S(1)} %get-tuple-element.153, f32[768]{0:T(1024)S(1)} %copy-done.30), channel_id=1, replica_groups=mesh['grp'=2,'dp'=4,'tp'=4] {'dp','tp'}, use_global_device_ids=true, to_apply=%region_20.21 | all-reduce | flops 1536 | bytes 12288 | tf_op jit(solution)/shard_map/psum | solution.py:179
  737.7 5.6 all-reduce.1
  746.6 17.6 %all-reduce.5.cloned.1.call-done = (f32[192,576]{1,0:T(8,128)}, f32[192,192]{1,0:T(8,128)}, f32[192,768]{1,0:T(8,128)}, f32[768,192]{0,1:T(8,128)}) async-done(((f32[192,576]{1,0:T(8,128)}, f32[192,192]{1,0:T(8,128)}, f32[192,768]{1,0:T(8,128)}, f32[768,192]{0,1:T(8,128)}), (f32[192,576]{1,0:T(8,128)}, f32[192,192]{1,0:T(8,128)}, f32[192,768]{1,0:T(8,128)}, ...) | async-done | bytes 1769488 | tf_op jit(solution)/shard_map/psum | solution.py:180
  (235 shorter events, 120.6 us)
Async XLA Ops:
  7.2 261.2 %copy-start = (bf16[768,768]{1,0:T(8,128)(2,1)S(1)}, bf16[768,768]{1,0:T(8,128)(2,1)}, u32[]{:S(2)}) copy-start(bf16[768,768]{1,0:T(8,128)(2,1)} %param.20) | copy-start | bytes 3538948
  7.2 37.4 %copy-start.33 = (bf16[768,576]{0,1:T(8,128)(2,1)S(1)}, bf16[768,576]{0,1:T(8,128)(2,1)}, u32[]{:S(2)}) copy-start(bf16[768,576]{0,1:T(8,128)(2,1)} %param.16) | copy-start | bytes 2654212
  7.2 37.3 %all-gather.5.cloned.1.call-start = ((), (), s32[]{:S(2)}) async-start(), calls=%async_computation.8 | async-start | bytes 3932160 | tf_op jit(solution)/shard_map/all_gather | solution.py:112
  13.1 192.5 %reduce-scatter.11.cloned.1.call-start = ((), (), s32[]{:S(2)}) async-start(), calls=%async_computation.9 | async-start | bytes 7864320 | tf_op jit(solution)/shard_map/reduce_scatter | solution.py:123
  140.2 6.9 copy-start.12
  147.1 58.5 %copy-start.10 = (bf16[512,768]{1,0:T(8,128)(2,1)S(1)}, bf16[512,768]{1,0:T(8,128)(2,1)}, u32[]{:S(2)}) copy-start(bf16[512,768]{1,0:T(8,128)(2,1)} %param.13) | copy-start | bytes 2359300
  147.1 61.3 %copy-start.24 = (f32[768]{0:T(1024)S(1)}, f32[768]{0:T(1024)}, u32[]{:S(2)}) copy-start(f32[768]{0:T(1024)} %param.18) | copy-start | bytes 9220
  147.1 91.2 %all-gather.7.cloned.1.call-start = ((), (), s32[]{:S(2)}) async-start(), calls=%async_computation.10 | async-start | bytes 3932160 | tf_op jit(solution)/shard_map/all_gather | solution.py:130
  208.4 37.3 %copy-start.28 = (f32[512]{0:T(512)}, f32[512]{0:T(512)S(1)}, u32[]{:S(2)}) copy-start(f32[512]{0:T(512)S(1)} %add_rsqrt_fusion) | copy-start | bytes 6148
  209.6 58.8 %all-gather.9.cloned.1.call-start = ((), (), s32[]{:S(2)}) async-start(), calls=%async_computation.12 | async-start | bytes 3932160 | tf_op jit(solution)/shard_map/all_gather | solution.py:143
  210.2 142.2 %reduce-scatter.15.cloned.1.call-start = ((), (), s32[]{:S(2)}) async-start(), calls=%async_computation.13 | async-start | bytes 7864320 | tf_op jit(solution)/shard_map/reduce_scatter | solution.py:150
  268.3 20.9 %copy-start.32 = (bf16[768,768]{1,0:T(8,128)(2,1)S(1)}, bf16[768,768]{1,0:T(8,128)(2,1)}, u32[]{:S(2)}) copy-start(bf16[768,768]{1,0:T(8,128)(2,1)} %param.19) | copy-start | bytes 3538948
  293.8 98.9 %reduce-scatter.13.cloned.1.call-start = ((), (), s32[]{:S(2)}) async-start(), calls=%async_computation.11 | async-start | bytes 3932160 | tf_op jit(solution)/shard_map/reduce_scatter | solution.py:136
  305.0 47.3 %copy-start.29 = (f32[512]{0:T(512)S(1)}, f32[512]{0:T(512)}, u32[]{:S(2)}) copy-start(f32[512]{0:T(512)} %copy-done.28) | copy-start | bytes 6148
  305.0 87.7 %copy-start.16 = (bf16[512,768]{1,0:T(8,128)(2,1)S(1)}, bf16[512,768]{1,0:T(8,128)(2,1)}, u32[]{:S(2)}) copy-start(bf16[512,768]{1,0:T(8,128)(2,1)} %param.21) | copy-start | bytes 2359300
  305.0 120.9 %all-gather.11.cloned.1.call-start = ((), (), s32[]{:S(2)}) async-start(), calls=%async_computation.14 | async-start | bytes 3932160 | tf_op jit(solution)/shard_map/all_gather | solution.py:158
  392.7 33.2 %copy-start.15 = (bf16[24,8,4,512]{3,1,2,0:T(8,128)(2,1)S(1)}, bf16[24,8,4,512]{3,1,2,0:T(8,128)(2,1)}, u32[]{:S(2)}) copy-start(bf16[24,8,4,512]{3,1,2,0:T(8,128)(2,1)} %copy-done.14) | copy-start | bytes 2359300
  397.3 208.5 %reduce-scatter.25.cloned.1.call-start = ((), (), s32[]{:S(2)}) async-start(), calls=%async_computation.19 | async-start | bytes 983040
  430.1 177.5 %reduce-scatter.23.cloned.1.call-start = ((), (), s32[]{:S(2)}) async-start(), calls=%async_computation.18 | async-start | bytes 2949120 | tf_op jit(solution)/shard_map/reduce_scatter | solution.py:177
  437.1 170.5 %reduce-scatter.21.cloned.1.call-start = ((), (), s32[]{:S(2)}) async-start(), calls=%async_computation.17 | async-start | bytes 2949120 | tf_op jit(solution)/shard_map/reduce_scatter | solution.py:176
  437.1 7.1 copy-start.21
  444.2 198.3 %reduce-scatter.19.cloned.1.call-start = ((), (), s32[]{:S(2)}) async-start(), calls=%async_computation.16 | async-start | bytes 2457600 | tf_op jit(solution)/shard_map/reduce_scatter | solution.py:174
  448.5 7.8 copy-start.4
  448.5 7.8 copy-start.7
  448.5 7.8 copy-start.18
  473.0 5.9 copy-start.2
  482.5 7.8 %copy-start.4 = (bf16[2048,3,64]{0,2,1:T(8,128)(2,1)}, bf16[2048,3,64]{0,2,1:T(8,128)(2,1)S(1)}, u32[]{:S(2)}) copy-start(bf16[2048,3,64]{0,2,1:T(8,128)(2,1)S(1)} %get-tuple-element.418) | copy-start | bytes 2359300 | tf_op jit(solution)/shard_map/while
  482.5 7.8 %copy-start.7 = (bf16[2048,3,64]{0,2,1:T(8,128)(2,1)}, bf16[2048,3,64]{0,2,1:T(8,128)(2,1)S(1)}, u32[]{:S(2)}) copy-start(bf16[2048,3,64]{0,2,1:T(8,128)(2,1)S(1)} %get-tuple-element.421) | copy-start | bytes 2359300 | tf_op jit(solution)/shard_map/while
  482.6 7.8 %copy-start.18 = (bf16[2048,3,64]{0,2,1:T(8,128)(2,1)}, bf16[2048,3,64]{0,2,1:T(8,128)(2,1)S(1)}, u32[]{:S(2)}) copy-start(bf16[2048,3,64]{0,2,1:T(8,128)(2,1)S(1)} %get-tuple-element.420) | copy-start | bytes 2359300 | tf_op jit(solution)/shard_map/while
  508.4 6.2 copy-start.2
  514.5 4.2 copy-start.19
  518.8 7.8 %copy-start.4 = (bf16[2048,3,64]{0,2,1:T(8,128)(2,1)}, bf16[2048,3,64]{0,2,1:T(8,128)(2,1)S(1)}, u32[]{:S(2)}) copy-start(bf16[2048,3,64]{0,2,1:T(8,128)(2,1)S(1)} %get-tuple-element.418) | copy-start | bytes 2359300 | tf_op jit(solution)/shard_map/while
  518.8 7.8 %copy-start.7 = (bf16[2048,3,64]{0,2,1:T(8,128)(2,1)}, bf16[2048,3,64]{0,2,1:T(8,128)(2,1)S(1)}, u32[]{:S(2)}) copy-start(bf16[2048,3,64]{0,2,1:T(8,128)(2,1)S(1)} %get-tuple-element.421) | copy-start | bytes 2359300 | tf_op jit(solution)/shard_map/while
  518.8 7.8 %copy-start.18 = (bf16[2048,3,64]{0,2,1:T(8,128)(2,1)}, bf16[2048,3,64]{0,2,1:T(8,128)(2,1)S(1)}, u32[]{:S(2)}) copy-start(bf16[2048,3,64]{0,2,1:T(8,128)(2,1)S(1)} %get-tuple-element.420) | copy-start | bytes 2359300 | tf_op jit(solution)/shard_map/while
  544.6 5.9 copy-start.2
  554.6 7.8 copy-start.4
  554.7 7.8 copy-start.7
  554.7 7.8 copy-start.18
  580.4 5.8 copy-start.2
  601.0 101.7 %reduce-scatter.17.cloned.1.call-start = ((), (), s32[]{:S(2)}) async-start(), calls=%async_computation.15 | async-start | bytes 7864320 | tf_op jit(solution)/shard_map/reduce_scatter | solution.py:165
  605.7 97.1 %copy-start.11 = (bf16[512,768]{1,0:T(8,128)(2,1)S(1)}, bf16[512,768]{1,0:T(8,128)(2,1)}, u32[]{:S(2)}) copy-start(bf16[512,768]{1,0:T(8,128)(2,1)} %param.13) | copy-start | bytes 2359300
  605.7 97.1 %copy-start.23 = (f32[512]{0:T(512)S(1)}, f32[512]{0:T(512)}, u32[]{:S(2)}) copy-start(f32[512]{0:T(512)} %copy-done.22) | copy-start | bytes 6148
  605.7 97.1 %copy-start.25 = (f32[768]{0:T(1024)S(1)}, f32[768]{0:T(1024)}, u32[]{:S(2)}) copy-start(f32[768]{0:T(1024)} %param.15) | copy-start | bytes 9220
  605.7 97.1 %copy-start.27 = (f32[512]{0:T(512)S(1)}, f32[512]{0:T(512)}, u32[]{:S(2)}) copy-start(f32[512]{0:T(512)} %copy-done.26) | copy-start | bytes 6148
  605.7 99.3 %copy-start.30 = (f32[768]{0:T(1024)S(1)}, f32[768]{0:T(1024)}, u32[]{:S(2)}) copy-start(f32[768]{0:T(1024)} %get-tuple-element.151) | copy-start | bytes 9220
  605.7 158.5 %all-reduce.5.cloned.1.call-start = ((), (), s32[]{:S(2)}) async-start(), calls=%async_computation.20 | async-start | bytes 3735552 | tf_op jit(solution)/shard_map/psum | solution.py:180
  702.7 40.6 %copy-start.13 = (f32[512,768]{1,0:T(8,128)S(1)}, f32[512,768]{1,0:T(8,128)}, u32[]{:S(2)}) copy-start(f32[512,768]{1,0:T(8,128)} %reduce-scatter.17.cloned.1.call-done) | copy-start | bytes 4718596
  743.4 28.2 %copy-start.1 = (bf16[768,768]{1,0:T(8,128)(2,1)S(1)}, bf16[768,768]{1,0:T(8,128)(2,1)}, u32[]{:S(2)}) copy-start(bf16[768,768]{1,0:T(8,128)(2,1)} %param.20) | copy-start | bytes 3538948
  (25 other events, 75.7 us)
Sparse Core Ops, SparseCore 0:
  13.3 31.2 all-gather.4
  147.2 58.3 reduce-scatter.10
  209.7 28.5 all-gather.6
  239.8 28.5 all-gather.8
  293.9 58.3 reduce-scatter.14
  354.7 37.9 reduce-scatter.12
  397.4 28.5 all-gather.10
  430.2 23.2 reduce-scatter.24
  456.0 47.2 reduce-scatter.22
  505.6 47.5 reduce-scatter.20
  601.1 41.3 reduce-scatter.18
  645.1 57.5 reduce-scatter.16
  705.8 58.3 all-reduce.4
where the time goes:
time: 788 us; the launch traced here: 778 us
  waiting for transfers between devices  366 us (46%)
  matrix products  224 us (28%)
  other arithmetic  88.1 us (11%)
  blocking collectives  38.3 us (5%)
  local copies, waits for them, and re-layouts  32.1 us (4%)
  between operations  15.4 us (2%)
  loops' own time  14 us (2%)
    reduce_scatter x1, waiting for transfers between devices, on_device(): lax.psum_scatter(jnp.einsum('tc,dc->td', picked, w_qkv, preferred_element...  60.2 us
    reduce_scatter x1, waiting for transfers between devices, on_device(): lax.psum_scatter(jnp.dot(picked, w_out, preferred_element_type=jnp.float3...  58.5 us
    reduce_scatter x1, waiting for transfers between devices, on_device(): lax.psum_scatter(jnp.einsum('tf,df->td', picked, w_up, preferred_element_...  47.2 us
    reduce_scatter x1, waiting for transfers between devices, on_device(): lax.psum_scatter(jnp.dot(picked, w_down, preferred_element_type=jnp.float...  37.2 us
    dot_general x8, matrix products, masked_scores(): jnp.einsum('qhd,khd->hqk', q_rows, key_rows, preferred_element_type=jnp.f...  36 us
    reduce_scatter x1, waiting for transfers between devices, on_device(): lax.psum_scatter(grad_qkv, 'dp', scatter_dimension=0, tiled=True)  35 us
    psum x1, blocking collectives, on_device(): lax.psum((gain_part_attn, gain_part_mlp), ('dp', 'tp'))  32.7 us
    all_gather x1, waiting for transfers between devices, on_device(): lax.all_gather(normed_attn.astype(jnp.bfloat16), 'tp', axis=0, tiled=True)  30.5 us
  transfers between devices with their start and end apart: 13, of which 10 were waited for; matrix products, arithmetic and copies ran while one was open for 24% of the time, Pallas kernels for 0%

commit v1 on v0

v1 whole, which is shorter than its diff:
```python
from functools import partial

import jax
import jax.numpy as jnp
from jax import lax
from jax.experimental import pallas as pl
from jax.experimental.pallas import tpu as pltpu
from jax.sharding import PartitionSpec as P

HD = 64
LANES = 128
IMAGE = 240
EXCLUDED = -1e30
MIB = 1024 * 1024
NT = (((1,), (1,)), ((), ()))
TN = (((0,), (0,)), ((), ()))

epsilon = 1e-06


def normalize(values, scaling):
    centred = values - jnp.mean(values, axis=1, keepdims=True)
    inverse = lax.rsqrt(jnp.mean(centred * centred, axis=1, keepdims=True) + epsilon)
    normed = centred * inverse
    return (normed * scaling, normed, inverse)


def restore(d_normed, normed, inverse, scaling):
    d_scaled = d_normed * scaling
    return inverse * (
        d_scaled
        - jnp.mean(d_scaled, axis=1, keepdims=True)
        - normed * jnp.mean(d_scaled * normed, axis=1, keepdims=True)
    )


def swap(value, distance, axis="tp"):
    size = lax.axis_size(axis)
    return lax.ppermute(value, axis, [(i, i ^ distance) for i in range(size)])


def add(left, right):
    return left.astype(jnp.float32) + right.astype(jnp.float32)


def gather_blocks(own):
    across = swap(own, 2)
    return [own, swap(own, 1), across, swap(across, 1)]


def scatter_blocks(parts):
    here = add(parts[0], swap(parts[1], 1))
    there = add(parts[2], swap(parts[3], 1)).astype(jnp.bfloat16)
    return here + swap(there, 2).astype(jnp.float32)


def attend_kernel(
    heads, bounds_ref, q_ref, k_ref, v_ref, id_q_ref, id_k_ref, out_ref, log_ref, turned, ids
):
    block = pl.program_id(0)
    width = q_ref.shape[0]

    @pl.when(block == 0)
    def _():
        for h in range(heads):
            value = v_ref[:, h * LANES : (h + 1) * LANES].astype(jnp.float32).T
            turned[h, :HD] = value[:HD].astype(jnp.bfloat16)
            turned[h, HD:] = jnp.ones((turned.shape[1] - HD, v_ref.shape[0]), jnp.bfloat16)
        ids[...] = jnp.broadcast_to(id_k_ref[...], ids.shape)

    id_q = id_q_ref[...]
    queries = [q_ref[:, h * LANES : (h + 1) * LANES] for h in range(heads)]

    def step(number, carry):
        at = pl.ds(pl.multiple_of((number ^ bounds_ref[0]) * width, width), width)
        mask = jnp.concatenate([ids[at, :]] * (width // LANES), axis=1) == id_q
        result = []
        for h in range(heads):
            largest, total = carry[h]
            scores = lax.dot_general(
                k_ref[at, h * LANES : (h + 1) * LANES],
                queries[h],
                NT,
                preferred_element_type=jnp.float32,
            )
            scores = jnp.where(mask, scores, EXCLUDED)
            top = jnp.maximum(largest, jnp.max(scores, axis=0, keepdims=True))
            exponent = jnp.exp(scores - top).astype(jnp.bfloat16)
            total = total * jnp.exp(largest - top) + jnp.dot(
                turned[h, :, at], exponent, preferred_element_type=jnp.float32
            )
            result.append((top, total))
        return tuple(result)

    start = tuple(
        (
            jnp.full((1, width), EXCLUDED, jnp.float32),
            jnp.zeros((turned.shape[1], width), jnp.float32),
        )
        for _ in range(heads)
    )
    result = lax.fori_loop(bounds_ref[1 + 2 * block], bounds_ref[2 + 2 * block], step, start)
    for h in range(heads):
        largest, total = result[h]
        denominator = total[HD : HD + 1]
        out_ref[:, h * HD : (h + 1) * HD] = (total[:HD] / denominator).T.astype(jnp.bfloat16)
        log_ref[h : h + 1, :] = largest + jnp.log(denominator)


def attend(qkv, image_id, bounds, heads):
    rows = qkv.shape[0]
    wide = heads * LANES
    width = rows // 4
    return pl.pallas_call(
        partial(attend_kernel, heads),
        grid_spec=pltpu.PrefetchScalarGridSpec(
            num_scalar_prefetch=1,
            grid=(4,),
            in_specs=[
                pl.BlockSpec((width, wide), lambda i, _: (i, 0)),
                pl.BlockSpec((rows, wide), lambda i, _: (0, 1)),
                pl.BlockSpec((rows, wide), lambda i, _: (0, 2)),
                pl.BlockSpec((1, width), lambda i, _: (0, i)),
                pl.BlockSpec((rows, 1), lambda i, _: (0, 0)),
            ],
            out_specs=[
                pl.BlockSpec((width, heads * HD), lambda i, _: (i, 0)),
                pl.BlockSpec((heads, width), lambda i, _: (0, i)),
            ],
            scratch_shapes=[
                pltpu.VMEM((heads, HD + 16, rows), jnp.bfloat16),
                pltpu.VMEM((rows, LANES), jnp.int32),
            ],
        ),
        out_shape=[
            jax.ShapeDtypeStruct((rows, heads * HD), jnp.bfloat16),
            jax.ShapeDtypeStruct((heads, rows), jnp.float32),
        ],
        compiler_params=pltpu.CompilerParams(vmem_limit_bytes=48 * MIB),
        cost_estimate=pl.CostEstimate(
            flops=heads * rows * rows * HD * 6, bytes_accessed=6 * MIB, transcendentals=0
        ),
        name="attend",
    )(bounds, qkv, qkv, qkv, image_id[None, :], image_id[:, None])


def attend_back_kernel(
    heads,
    bounds_ref,
    q_ref,
    k_ref,
    v_ref,
    grad_ref,
    out_ref,
    log_ref,
    id_q_ref,
    id_k_ref,
    d_ref,
    turned,
    ids,
    d_keys,
    d_values,
):
    block = pl.program_id(0)
    width = q_ref.shape[0]

    @pl.when(block == 0)
    def _():
        for h in range(heads):
            key = k_ref[:, h * LANES : (h + 1) * LANES].astype(jnp.float32).T
            turned[h] = key[:HD].astype(jnp.bfloat16)
        ids[...] = jnp.broadcast_to(id_k_ref[...], ids.shape)
        d_keys[...] = jnp.zeros_like(d_keys)
        d_values[...] = jnp.zeros_like(d_values)

    id_q = id_q_ref[...]
    ones = jnp.ones((8, HD), jnp.float32)
    queries = [q_ref[:, h * LANES : (h + 1) * LANES] for h in range(heads)]
    grads = [grad_ref[:, h * HD : (h + 1) * HD] for h in range(heads)]
    logs = [log_ref[h : h + 1, :] for h in range(heads)]
    inner = []
    for h in range(heads):
        product = grads[h].astype(jnp.float32) * out_ref[:, h * HD : (h + 1) * HD].astype(
            jnp.float32
        )
        inner.append(
            lax.dot_general(
                ones,
                product,
                NT,
                precision=lax.Precision.HIGHEST,
                preferred_element_type=jnp.float32,
            )[:1]
        )

    def step(number, carry):
        at = pl.ds(pl.multiple_of((number ^ bounds_ref[0]) * width, width), width)
        mask = jnp.concatenate([ids[at, :]] * (width // LANES), axis=1) == id_q
        result = []
        for h in range(heads):
            scores = lax.dot_general(
                k_ref[at, h * LANES : (h + 1) * LANES],
                queries[h],
                NT,
                preferred_element_type=jnp.float32,
            )
            probs = jnp.where(mask, jnp.exp(scores - logs[h]), 0.0)
            d_probs = lax.dot_general(
                v_ref[at, h * LANES : h * LANES + HD],
                grads[h],
                NT,
                preferred_element_type=jnp.float32,
            )
            d_scores = (probs * (d_probs - inner[h])).astype(jnp.bfloat16)
            d_values[h, at, :] += jnp.dot(
                probs.astype(jnp.bfloat16), grads[h], preferred_element_type=jnp.float32
            )
            d_keys[h, at, :] += jnp.dot(d_scores, queries[h], preferred_element_type=jnp.float32)[
                :, :HD
            ]
            result.append(
                carry[h]
                + jnp.dot(turned[h, :, at], d_scores, preferred_element_type=jnp.float32)
            )
        return tuple(result)

    start = tuple(jnp.zeros((HD, width), jnp.float32) for _ in range(heads))
    result = lax.fori_loop(bounds_ref[1 + 2 * block], bounds_ref[2 + 2 * block], step, start)
    here = pl.ds(pl.multiple_of(block * width, width), width)
    for h in range(heads):
        d_ref[here, 3 * h * HD : (3 * h + 1) * HD] = (result[h] * 0.125).T.astype(jnp.bfloat16)

    @pl.when(block == pl.num_programs(0) - 1)
    def _():
        for h in range(heads):
            d_ref[:, (3 * h + 1) * HD : (3 * h + 2) * HD] = d_keys[h].astype(jnp.bfloat16)
            d_ref[:, (3 * h + 2) * HD : (3 * h + 3) * HD] = d_values[h].astype(jnp.bfloat16)


def attend_back(qkv, d_heads, heads_out, log_total, image_id, bounds, heads):
    rows = qkv.shape[0]
    wide = heads * LANES
    width = rows // 4
    return pl.pallas_call(
        partial(attend_back_kernel, heads),
        grid_spec=pltpu.PrefetchScalarGridSpec(
            num_scalar_prefetch=1,
            grid=(4,),
            in_specs=[
                pl.BlockSpec((width, wide), lambda i, _: (i, 0)),
                pl.BlockSpec((rows, wide), lambda i, _: (0, 1)),
                pl.BlockSpec((rows, wide), lambda i, _: (0, 2)),
                pl.BlockSpec((width, heads * HD), lambda i, _: (i, 0)),
                pl.BlockSpec((width, heads * HD), lambda i, _: (i, 0)),
                pl.BlockSpec((heads, width), lambda i, _: (0, i)),
                pl.BlockSpec((1, width), lambda i, _: (0, i)),
                pl.BlockSpec((rows, 1), lambda i, _: (0, 0)),
            ],
            out_specs=pl.BlockSpec((rows, 3 * heads * HD), lambda i, _: (0, 0)),
            scratch_shapes=[
                pltpu.VMEM((heads, HD, rows), jnp.bfloat16),
                pltpu.VMEM((rows, LANES), jnp.int32),
                pltpu.VMEM((heads, rows, HD), jnp.float32),
                pltpu.VMEM((heads, rows, HD), jnp.float32),
            ],
        ),
        out_shape=jax.ShapeDtypeStruct((rows, 3 * heads * HD), jnp.bfloat16),
        compiler_params=pltpu.CompilerParams(vmem_limit_bytes=48 * MIB),
        cost_estimate=pl.CostEstimate(
            flops=heads * rows * rows * HD * 10, bytes_accessed=10 * MIB, transcendentals=0
        ),
        name="attend_back",
    )(bounds, qkv, qkv, qkv, d_heads, heads_out, log_total, image_id[None, :], image_id[:, None])


def mlp_kernel(
    steps,
    first,
    x_a_ref,
    x_b_ref,
    g_a_ref,
    g_b_ref,
    up_ref,
    down_ref,
    *refs,
):
    if first:
        y_a_ref, y_b_ref, m_a_ref, m_b_ref, d_up_ref, d_down_ref = refs
    else:
        old_up_ref, old_down_ref, y_a_ref, y_b_ref, m_a_ref, m_b_ref, d_up_ref, d_down_ref = refs
    number = pl.program_id(0)

    @pl.when(number == 0)
    def _():
        if first:
            d_up_ref[...] = jnp.zeros_like(d_up_ref)
            d_down_ref[...] = jnp.zeros_like(d_down_ref)
        else:
            d_up_ref[...] = old_up_ref[...]
            d_down_ref[...] = old_down_ref[...]

    def rows(x_ref, g_ref, y_ref, m_ref):
        mlp_in = x_ref[...]
        out_grads = g_ref[...]
        pre_act = jnp.dot(mlp_in, up_ref[...], preferred_element_type=jnp.float32)
        d_act = lax.dot_general(
            out_grads, down_ref[...], NT, preferred_element_type=jnp.float32
        )
        below = 0.5 + 0.5 * lax.erf(pre_act * 0.7071067811865476)
        density = 0.3989422804014327 * jnp.exp(-0.5 * pre_act * pre_act)
        act = (pre_act * below).astype(jnp.bfloat16)
        d_pre = (d_act * (below + pre_act * density)).astype(jnp.bfloat16)
        y_ref[...] = jnp.dot(act, down_ref[...], preferred_element_type=jnp.float32).astype(
            jnp.bfloat16
        )
        m_ref[...] = lax.dot_general(
            d_pre, up_ref[...], NT, preferred_element_type=jnp.float32
        ).astype(jnp.bfloat16)
        d_up_ref[...] += lax.dot_general(mlp_in, d_pre, TN, preferred_element_type=jnp.float32)
        d_down_ref[...] += lax.dot_general(out_grads, act, TN, preferred_element_type=jnp.float32)

    @pl.when(number < steps)
    def _():
        rows(x_a_ref, g_a_ref, y_a_ref, m_a_ref)

    @pl.when(number >= steps)
    def _():
        rows(x_b_ref, g_b_ref, y_b_ref, m_b_ref)


def mlp(x_a, x_b, g_a, g_b, skip, w_up, w_down, sums):
    length, model = x_a.shape
    hidden = w_up.shape[1]
    tile = min(256, length)
    steps = length // tile
    first = sums is None

    def in_a(i):
        return (jnp.minimum(i, steps - 1), 0)

    def in_b(i):
        return (jnp.maximum(i - steps, 0), 0)

    def grads_a(i):
        return (jnp.minimum(i, steps - 1) + skip // tile, 0)

    def grads_b(i):
        return (jnp.maximum(i - steps, 0) + skip // tile, 0)

    def whole(shape):
        return pl.BlockSpec(shape, lambda i: (0, 0))

    rows = jax.ShapeDtypeStruct((length, model), jnp.bfloat16)
    totals = [
        jax.ShapeDtypeStruct((model, hidden), jnp.float32),
        jax.ShapeDtypeStruct((model, hidden), jnp.float32),
    ]
    total_specs = [whole((model, hidden)), whole((model, hidden))]
    return pl.pallas_call(
        partial(mlp_kernel, steps, first),
        grid=(2 * steps,),
        in_specs=[
            pl.BlockSpec((tile, model), in_a),
            pl.BlockSpec((tile, model), in_b),
            pl.BlockSpec((tile, model), grads_a),
            pl.BlockSpec((tile, model), grads_b),
            whole((model, hidden)),
            whole((hidden, model)),
        ]
        + ([] if first else total_specs),
        out_specs=[
            pl.BlockSpec((tile, model), in_a),
            pl.BlockSpec((tile, model), in_b),
            pl.BlockSpec((tile, model), in_a),
            pl.BlockSpec((tile, model), in_b),
        ]
        + total_specs,
        out_shape=[rows, rows, rows, rows] + totals,
        input_output_aliases={} if first else {6: 4, 7: 5},
        compiler_params=pltpu.CompilerParams(vmem_limit_bytes=56 * MIB),
        cost_estimate=pl.CostEstimate(
            flops=2 * length * model * hidden * 12, bytes_accessed=16 * MIB, transcendentals=0
        ),
        name="mlp",
    )(x_a, x_b, g_a, g_b, w_up, w_down, *([] if first else sums))


def reduce_rows(arrays):
    count = lax.axis_size("dp")
    index = lax.axis_index("dp")
    widths = [a.shape[1] for a in arrays]
    kept = [a.reshape(count, a.shape[0] // count, a.shape[1]) for a in arrays]
    distance = 1
    while distance < count:
        bit = (index // distance) % 2
        pairs = [k.reshape(-1, 2, *k.shape[1:]) for k in kept]
        sent = jnp.concatenate(
            [
                lax.dynamic_index_in_dim(p, 1 - bit, 1, keepdims=False).astype(jnp.bfloat16)
                for p in pairs
            ],
            axis=2,
        )
        got = swap(sent, distance, "dp")
        first = 0
        summed = []
        for p, w in zip(pairs, widths):
            mine = lax.dynamic_index_in_dim(p, bit, 1, keepdims=False)
            summed.append(add(mine, got[:, :, first : first + w]))
            first += w
        kept = summed
        distance *= 2
    mine = jnp.concatenate([k[0].astype(jnp.bfloat16) for k in kept], axis=1)
    size = lax.axis_size("grp")
    total = mine
    for shift in range(1, size):
        total = add(total, lax.ppermute(mine, "grp", [(i, i ^ shift) for i in range(size)]))
    first = 0
    result = []
    for w in widths:
        result.append(total[:, first : first + w])
        first += w
    return result


def on_device(tokens, patch_side, gain_attn, w_qkv, w_out, gain_mlp, w_up, w_down, cotangent):
    rows, model = tokens.shape
    place = lax.axis_index("tp")
    group_rows = 4 * rows
    half = rows // 2
    heads = w_out.shape[0] // HD

    activations = tokens.astype(jnp.float32)
    normed_attn, unit_attn, inverse_attn = normalize(activations, gain_attn)
    attn_in = jnp.concatenate(gather_blocks(normed_attn.astype(jnp.bfloat16)), axis=0)

    cells = (IMAGE // patch_side[0]) ** 2
    full = group_rows // cells
    order = place ^ jnp.arange(4, dtype=jnp.int32)
    positions = (order[:, None] * rows + jnp.arange(rows, dtype=jnp.int32)).reshape(-1)
    image_id = jnp.minimum(positions // cells, full)
    first_id = jnp.minimum(order * rows // cells, full)
    last_id = jnp.minimum((order * rows + rows - 1) // cells, full)
    low = first_id * cells // rows
    stop = jnp.where(last_id == full, group_rows, (last_id + 1) * cells)
    high = (stop + rows - 1) // rows
    bounds = jnp.concatenate([place[None], jnp.stack([low, high], axis=1).reshape(-1)])

    by_head = w_qkv.reshape(model, heads, 3, HD)
    by_head = by_head * jnp.array([0.125, 1.0, 1.0], jnp.bfloat16)[:, None]
    spread = jnp.pad(by_head.transpose(0, 2, 1, 3), ((0, 0), (0, 0), (0, 0), (0, LANES - HD)))
    spread = spread.reshape(model, 3 * heads * LANES)
    qkv = jnp.dot(attn_in, spread, preferred_element_type=jnp.float32).astype(jnp.bfloat16)

    heads_out, log_total = attend(qkv, image_id, bounds, heads)

    w_outs = gather_blocks(w_out)
    pieces = [heads_out[j * rows : (j + 1) * rows] for j in range(4)]
    mine = [pieces[0]] + [swap(pieces[j], j) for j in range(1, 4)]
    branch = jnp.dot(mine[0], w_outs[0], preferred_element_type=jnp.float32)
    for j in range(1, 4):
        branch = branch + jnp.dot(mine[j], w_outs[j], preferred_element_type=jnp.float32)
    resid = activations + branch

    normed_mlp, unit_mlp, inverse_mlp = normalize(resid, gain_mlp)
    mlp_in = normed_mlp.astype(jnp.bfloat16)
    out_grads = gather_blocks(cotangent)
    near = swap(mlp_in, 1)
    across = [swap(mlp_in[:half], 2), swap(mlp_in[half:], 2)]
    diagonal = [swap(a, 1) for a in across]

    y_0, y_1, m_0, m_1, *sums = mlp(
        mlp_in, near, out_grads[0], out_grads[1], 0, w_up, w_down, None
    )
    far_y = []
    far_m = []
    for k in range(2):
        y_2, y_3, m_2, m_3, *sums = mlp(
            across[k], diagonal[k], out_grads[2], out_grads[3], k * half, w_up, w_down, sums
        )
        far_m.append(swap(add(m_2, swap(m_3, 1)).astype(jnp.bfloat16), 2))
        far_y.append((y_2, y_3))
    d_up, d_down = sums
    d_mlp_in = add(add(m_0, swap(m_1, 1)), jnp.concatenate(far_m, axis=0))
    d_resid = cotangent.astype(jnp.float32) + restore(d_mlp_in, unit_mlp, inverse_mlp, gain_mlp)

    d_branch = d_resid.astype(jnp.bfloat16)
    d_pieces = [
        lax.dot_general(d_branch, w, NT, preferred_element_type=jnp.float32).astype(jnp.bfloat16)
        for w in w_outs
    ]
    d_heads = [d_pieces[0]] + [swap(d_pieces[j], j) for j in range(1, 4)]
    d_heads = jnp.concatenate(d_heads, axis=0)

    mixed = scatter_blocks(
        [
            y_0,
            y_1,
            jnp.concatenate([far_y[0][0], far_y[1][0]], axis=0),
            jnp.concatenate([far_y[0][1], far_y[1][1]], axis=0),
        ]
    )
    mixed_rows = (resid + mixed).astype(jnp.bfloat16)

    d_out = scatter_blocks(
        [
            lax.dot_general(d_branch, h, TN, preferred_element_type=jnp.float32).astype(
                jnp.bfloat16
            )
            for h in mine
        ]
    )
    grad_up, grad_down, grad_out = reduce_rows([d_up, d_down, d_out])

    d_qkv = attend_back(qkv, d_heads, heads_out, log_total, image_id, bounds, heads)
    d_w_qkv = lax.dot_general(attn_in, d_qkv, TN, preferred_element_type=jnp.float32)
    (grad_qkv,) = reduce_rows([d_w_qkv])
    d_attn_in = scatter_blocks(
        [
            lax.dot_general(
                d_qkv[j * rows : (j + 1) * rows], w_qkv, NT, preferred_element_type=jnp.float32
            ).astype(jnp.bfloat16)
            for j in range(4)
        ]
    )
    input_grad = d_resid + restore(d_attn_in, unit_attn, inverse_attn, gain_attn)

    gain_parts = jnp.stack(
        [
            jnp.sum(d_w_qkv * w_qkv.astype(jnp.float32), axis=1) / gain_attn,
            jnp.sum(d_up * w_up.astype(jnp.float32), axis=1) / gain_mlp,
        ]
    )
    grad_gains = lax.psum(gain_parts, ("grp", "dp", "tp"))
    return (
        mixed_rows,
        input_grad,
        grad_gains[0],
        grad_qkv,
        grad_out.T,
        grad_gains[1],
        grad_up,
        grad_down.T,
    )


def solution(mesh):
    in_specs = (
        P(("grp", "dp", "tp"), None),
        P(("grp", "dp")),
        P(),
        P(None, "tp"),
        P("tp", None),
        P(),
        P(None, "tp"),
        P("tp", None),
        P(("grp", "dp", "tp"), None),
    )
    out_specs = (
        P(("grp", "dp", "tp"), None),
        P(("grp", "dp", "tp"), None),
        P(),
        P("dp", "tp"),
        P("tp", "dp"),
        P(),
        P("dp", "tp"),
        P("tp", "dp"),
    )
    return jax.shard_map(
        on_device, mesh=mesh, in_specs=in_specs, out_specs=out_specs, check_vma=False
    )
```

time: 788 us -> 406 us (0.52)
  waiting for transfers between devices: 366 us -> 123 us
  matrix products: 224 us -> 35.9 us
  Pallas kernels: 0 us -> 90.7 us
  other arithmetic: 88.1 us -> 27.1 us
  starting transfers between devices: 1.17 us -> 40 us
  loops' own time: 14 us -> 0 us
  between operations: 15.4 us -> 2.28 us
  blocking collectives: 38.3 us -> 50.1 us
    reduce_scatter x7 -> x0, waiting for transfers between devices: 238 us -> none  [the longest x1 60.2 us: on_device(): lax.psum_scatter(jnp.einsum('tc,dc->td', picked, w_qkv, preferred_element...]
    dot_general x39 -> x18, matrix products: 220 us -> 35.9 us  [the longest x4 9.05 us: on_device(): lax.dot_general(d_qkv[j * rows:(j + 1) * rows], w_qkv, NT, preferred_elem...]
    ppermute x0 -> x40, waiting for transfers between devices: none -> 123 us  [the longest x38 110 us: swap(): return lax.ppermute(value, axis, [(i, i ^ distance) for i in range(size)])]
    all_gather x4 -> x0, waiting for transfers between devices: 109 us -> none  [the longest x1 30.5 us: on_device(): lax.all_gather(normed_attn.astype(jnp.bfloat16), 'tp', axis=0, tiled=True)]
    pallas_call x0 -> x5, Pallas kernels: none -> 90.7 us  [the longest x3 35.4 us: mlp(): pl.pallas_call(partial(mlp_kernel, steps, first), grid=(2 * steps,), in_s...]
    ppermute x0 -> x40, starting transfers between devices: none -> 40 us  [the longest x38 36.8 us: swap(): return lax.ppermute(value, axis, [(i, i ^ distance) for i in range(size)])]
    convert_element_type x7 -> x8, other arithmetic: 35.6 us -> 5.71 us  [the longest x1 3.64 us: on_device(): d_branch = d_resid.astype(jnp.bfloat16)]
    reduce_sum x6 -> x2, other arithmetic: 32.4 us -> 2.79 us  [the longest x1 2.04 us: on_device(): jnp.sum(d_up * w_up.astype(jnp.float32), axis=1) / gain_mlp]
  transfers between devices with their start and end apart: 13 -> 40, of which waited for: 10 -> 15; matrix products, arithmetic and copies ran while one was open for 24% -> 19% of each run, Pallas kernels for 0% -> 23%
where the time goes in v1:
time: 406 us; the launch traced here: 399 us
  waiting for transfers between devices  123 us (30%)
  Pallas kernels  90.7 us (22%)
  blocking collectives  50.1 us (12%)
  starting transfers between devices  40 us (10%)
  matrix products  35.9 us (9%)
  local copies, waits for them, and re-layouts  29.7 us (7%)
  other arithmetic  27.1 us (7%)
    ppermute x38, waiting for transfers between devices, swap(): return lax.ppermute(value, axis, [(i, i ^ distance) for i in range(size)])  110 us
    psum x1, blocking collectives, on_device(): grad_gains = lax.psum(gain_parts, ('grp', 'dp', 'tp'))  50.1 us
    ppermute x38, starting transfers between devices, swap(): return lax.ppermute(value, axis, [(i, i ^ distance) for i in range(size)])  36.8 us
    pallas_call x3, Pallas kernels, mlp(): pl.pallas_call(partial(mlp_kernel, steps, first), grid=(2 * steps,), in_s...  35.4 us
    pallas_call x1, Pallas kernels, attend_back(): pl.pallas_call(partial(attend_back_kernel, heads), grid_spec=pltpu.Prefet...  33 us
    pallas_call x1, Pallas kernels, attend(): pl.pallas_call(partial(attend_kernel, heads), grid_spec=pltpu.PrefetchSca...  22.3 us
    ppermute x2, waiting for transfers between devices, reduce_rows(): lax.ppermute(mine, 'grp', [(i, i ^ shift) for i in range(size)])  13.5 us
    dot_general x4, matrix products, on_device(): lax.dot_general(d_qkv[j * rows:(j + 1) * rows], w_qkv, NT, preferred_elem...  9.05 us
  transfers between devices with their start and end apart: 40, of which 15 were waited for; matrix products, arithmetic and copies ran while one was open for 19% of the time, Pallas kernels for 23%

profile of v1, /device:TPU:0, one launch (start us, length us, event | category | flops | bytes accessed | tf_op | source)
XLA Modules:
  0.0 399.1 jit_solution(8608171459217659518)
XLA Ops:
  1.2 2.6 collective-permute-start.6
  11.5 17.1 %collective-permute-done.1 = bf16[512,768]{1,0:T(8,128)(2,1)} collective-permute-done((bf16[512,768]{1,0:T(8,128)(2,1)}, bf16[512,768]{1,0:T(8,128)(2,1)}, u32[]{:S(2)}, u32[]{:S(2)}) %collective-permute-start.1) | collective-permute-done | bytes 786464 | tf_op jit(solution)/shard_map/ppermute | solution.py:39
  28.8 1.8 collective-permute-start.14
  32.0 8.1 %convolution_convert_fusion.q_ref.k_ref.v_ref = bf16[2048,1152]{1,0:T(8,128)(2,1)} fusion(bf16[768,1152]{0,1:T(8,128)(2,1)S(1)} %bitcast.99, bf16[512,768]{1,0:T(8,128)(2,1)S(1)} %collective-permute-done.2, bf16[512,768]{1,0:T(8,128)(2,1)} %collective-permute-done.1, bf16[512,768]{1,0:T(8,128)(2,1)} %collective-permute-done, bf16[512,768]{1,0:T(8,128)(2,1)} %fusion.5), kind=kOutput, calls=%fused_computation | convolution fusion | flops 3638820864 | bytes 9633792 | tf_op jit(solution)/shard_map/dot_general | solution.py:453
  40.1 22.3 %attend.1 = (bf16[2048,192]{1,0:T(8,128)(2,1)S(1)}, f32[3,2048]{1,0:T(4,128)S(1)}) custom-call(s32[9]{0:T(128)S(1)} %pad_add_fusion.1.bounds_ref, bf16[2048,1152]{1,0:T(8,128)(2,1)} %convolution_convert_fusion.q_ref.k_ref.v_ref, bf16[2048,1152]{1,0:T(8,128)(2,1)} %convolution_convert_fusion.q_ref.k_ref.v_ref, ...), custom_call_target="tpu_custom_call" | custom-call | flops 4831838208 | bytes 6291456 | tf_op jit(solution)/shard_map/attend/pallas_call | solution.py:114
  62.5 1.8 collective-permute-start.5
  64.6 6.2 %collective-permute-done.5 = bf16[512,192]{1,0:T(8,128)(2,1)S(1)} collective-permute-done((bf16[512,192]{1,0:T(8,128)(2,1)S(1)}, bf16[512,192]{1,0:T(8,128)(2,1)S(1)}, u32[]{:S(2)}, u32[]{:S(2)}) %collective-permute-start.5) | collective-permute-done | bytes 196640 | tf_op jit(solution)/shard_map/ppermute | solution.py:39
  72.3 1.8 collective-permute-start.7
  75.6 4.9 %collective-permute-done.7 = bf16[512,192]{1,0:T(8,128)(2,1)S(1)} collective-permute-done((bf16[512,192]{1,0:T(8,128)(2,1)S(1)}, bf16[512,192]{1,0:T(8,128)(2,1)S(1)}, u32[]{:S(2)}, u32[]{:S(2)}) %collective-permute-start.7) | collective-permute-done | bytes 196640 | tf_op jit(solution)/shard_map/ppermute | solution.py:39
  83.6 1.7 collective-permute-start.12
  85.6 10.2 %collective-permute-done.12.x_a_ref = bf16[256,768]{1,0:T(8,128)(2,1)} collective-permute-done((bf16[256,768]{1,0:T(8,128)(2,1)}, bf16[256,768]{1,0:T(8,128)(2,1)}, u32[]{:S(2)}, u32[]{:S(2)}) %collective-permute-start.12) | collective-permute-done | bytes 393248 | tf_op jit(solution)/shard_map/ppermute | solution.py:39
  95.9 7.7 %collective-permute-done.16.x_a_ref = bf16[256,768]{1,0:T(8,128)(2,1)} collective-permute-done((bf16[256,768]{1,0:T(8,128)(2,1)}, bf16[256,768]{1,0:T(8,128)(2,1)}, u32[]{:S(2)}, u32[]{:S(2)}) %collective-permute-start.16) | collective-permute-done | bytes 393248 | tf_op jit(solution)/shard_map/ppermute | solution.py:39
  103.6 13.5 %mlp.3 = (bf16[512,768]{1,0:T(8,128)(2,1)}, bf16[512,768]{1,0:T(8,128)(2,1)}, bf16[512,768]{1,0:T(8,128)(2,1)}, bf16[512,768]{1,0:T(8,128)(2,1)}, f32[768,768]{1,0:T(8,128)}, /*index=5*/f32[768,768]{1,0:T(8,128)}) custom-call(bf16[512,768]{1,0:T(8,128)(2,1)} %copy-done.9, bf16[512,768]{1,0:T(8,128)(2,1)} %collective-permute-done.9.x_b_ref, ...), custom_call_target="tpu_custom_call" | custom-call | flops 7247757312 | bytes 16777216 | tf_op jit(solution)/shard_map/mlp/pallas_call | solution.py:359
  118.4 11.2 %mlp.4 = (bf16[256,768]{1,0:T(8,128)(2,1)}, bf16[256,768]{1,0:T(8,128)(2,1)}, bf16[256,768]{1,0:T(8,128)(2,1)}, bf16[256,768]{1,0:T(8,128)(2,1)}, f32[768,768]{1,0:T(8,128)}, /*index=5*/f32[768,768]{1,0:T(8,128)}) custom-call(bf16[256,768]{1,0:T(8,128)(2,1)} %collective-permute-done.12.x_a_ref, ...), custom_call_target="tpu_custom_call", output_to_operand_aliasing={{4}: (6, {}), {5}: (7, {})} | custom-call | flops 3623878656 | bytes 16777216 | tf_op jit(solution)/shard_map/mlp/pallas_call | solution.py:359
  130.9 10.8 %mlp.5 = (bf16[256,768]{1,0:T(8,128)(2,1)}, bf16[256,768]{1,0:T(8,128)(2,1)}, bf16[256,768]{1,0:T(8,128)(2,1)}, bf16[256,768]{1,0:T(8,128)(2,1)}, f32[768,768]{1,0:T(8,128)}, /*index=5*/f32[768,768]{1,0:T(8,128)}) custom-call(bf16[256,768]{1,0:T(8,128)(2,1)} %collective-permute-done.16.x_a_ref, ...), custom_call_target="tpu_custom_call", output_to_operand_aliasing={{4}: (6, {}), {5}: (7, {})} | custom-call | flops 3623878656 | bytes 16777216 | tf_op jit(solution)/shard_map/mlp/pallas_call | solution.py:359
  143.4 2.0 multiply_reduce_fusion
  145.5 1.8 collective-permute-start.22
  147.8 2.1 fusion.23
  150.2 1.8 collective-permute-start.19
  152.0 2.1 fusion.22
  154.2 3.4 collective-permute-done.22
  157.6 8.4 %collective-permute-done.24 = bf16[256,768]{1,0:T(8,128)(2,1)S(1)} collective-permute-done((bf16[256,768]{1,0:T(8,128)(2,1)S(1)}, bf16[256,768]{1,0:T(8,128)(2,1)S(1)}, u32[]{:S(2)}, u32[]{:S(2)}) %collective-permute-start.24) | collective-permute-done | bytes 393248 | tf_op jit(solution)/shard_map/ppermute | solution.py:39
  166.8 15.3 %collective-permute-done.19 = bf16[512,768]{1,0:T(8,128)(2,1)S(1)} collective-permute-done((bf16[512,768]{1,0:T(8,128)(2,1)S(1)}, bf16[512,768]{1,0:T(8,128)(2,1)S(1)}, u32[]{:S(2)}, u32[]{:S(2)}) %collective-permute-start.19) | collective-permute-done | bytes 786464 | tf_op jit(solution)/shard_map/ppermute | solution.py:39
  182.1 3.6 fusion.48
  192.3 1.8 copy.66
  197.1 2.0 convolution_convert_fusion.7
  200.1 3.6 collective-permute-done.27
  203.8 5.9 %collective-permute-done.26 = bf16[512,192]{1,0:T(8,128)(2,1)S(1)} collective-permute-done((bf16[512,192]{1,0:T(8,128)(2,1)}, bf16[512,192]{1,0:T(8,128)(2,1)S(1)}, u32[]{:S(2)}, u32[]{:S(2)}) %collective-permute-start.26) | collective-permute-done | bytes 196640 | tf_op jit(solution)/shard_map/ppermute | solution.py:39
  209.9 33.0 %attend_back.1 = bf16[2048,576]{1,0:T(8,128)(2,1)S(1)} custom-call(s32[9]{0:T(128)S(1)} %pad_add_fusion.1.bounds_ref, bf16[2048,1152]{1,0:T(8,128)(2,1)} %convolution_convert_fusion.q_ref.k_ref.v_ref, bf16[2048,1152]{1,0:T(8,128)(2,1)} %convolution_convert_fusion.q_ref.k_ref.v_ref, bf16[2048,1152]{1,0:T(8,128)(2,1)} %convolution_convert_fusion.q_ref.k_ref.v_ref, ...), custom_call_target="tpu_custom_call" | custom-call | flops 8053063680 | bytes 10485760 | tf_op jit(solution)/shard_map/attend_back/pallas_call | solution.py:244
  243.0 5.9 %multiply_reduce_fusion.1 = (f32[768]{0:T(1024)S(1)}, f32[768,576]{0,1:T(8,128)}) fusion(bf16[768,576]{0,1:T(8,128)(2,1)S(1)} %copy-done.19, bf16[2048,576]{1,0:T(8,128)(2,1)S(1)} %attend_back.1, bf16[512,768]{1,0:T(8,128)(2,1)S(1)} %copy-done.31, bf16[512,768]{1,0:T(8,128)(2,1)} %collective-permute-done.1, bf16[512,768]{1,0:T(8,128)(2,1)} %collective-permute-done, ...), kind=kOutput, calls=%fused_computation.11 | convolution fusion | flops 1825848576 | bytes 8162304 | tf_op jit(solution)/shard_map/dot_general | solution.py:516
  250.2 1.7 convolution_convert_fusion.3
  251.9 3.0 copy.68
  254.9 2.0 fusion.25
  261.7 2.0 copy.76
  263.7 2.6 pad_maximum_fusion.1
  267.8 2.8 convolution_convert_fusion.1
  271.3 2.1 bitcast_add_fusion.2
  273.3 1.8 dynamic-slice_convert_fusion.3
  275.1 10.7 %collective-permute-start.32 = (bf16[1,192,576]{2,1,0:T(8,128)(2,1)}, bf16[1,192,576]{2,1,0:T(8,128)(2,1)}, u32[]{:S(2)}, u32[]{:S(2)}) collective-permute-start(bf16[1,192,576]{2,1,0:T(8,128)(2,1)} %dynamic-slice_convert_fusion.3), channel_id=1, source_target_pairs={{0,8},{4,12},{8,0},{12,4},{1,9},{5,13},{9,1},{13,5},{2,10},{6,14},... | collective-permute-start | bytes 663560 | tf_op jit(solution)/shard_map/ppermute | solution.py:39
  285.8 50.1 %psum.7 = f32[2,768]{1,0:T(2,128)S(1)} all-reduce(f32[2,768]{1,0:T(2,128)S(1)} %pad_maximum_fusion.8), channel_id=1, replica_groups=mesh['grp'=2,'dp'=4,'tp'=4] {'grp','dp','tp'}, use_global_device_ids=true, to_apply=%region_10.11 | all-reduce | flops 1536 | bytes 12288 | tf_op jit(solution)/shard_map/psum | solution.py:534
  339.4 2.3 collective-permute-start.33
  341.8 2.2 add_convert_fusion
  344.7 2.0 bitcast_add_fusion.1
  350.6 10.8 %collective-permute-done.30 = bf16[512,768]{1,0:T(8,128)(2,1)S(1)} collective-permute-done((bf16[512,768]{1,0:T(8,128)(2,1)S(1)}, bf16[512,768]{1,0:T(8,128)(2,1)S(1)}, u32[]{:S(2)}, u32[]{:S(2)}) %collective-permute-start.30) | collective-permute-done | bytes 786464 | tf_op jit(solution)/shard_map/ppermute | solution.py:39
  361.4 2.4 fusion.32
  363.8 15.3 %collective-permute-done.38 = bf16[1,192,1728]{2,1,0:T(8,128)(2,1)S(1)} collective-permute-done((bf16[1,192,1728]{2,1,0:T(8,128)(2,1)S(1)}, bf16[1,192,1728]{2,1,0:T(8,128)(2,1)S(1)}, u32[]{:S(2)}, u32[]{:S(2)}) %collective-permute-start.38) | collective-permute-done | bytes 663584 | tf_op jit(solution)/shard_map/ppermute | solution.py:39
  380.3 3.0 fusion.9
  383.3 13.5 %collective-permute-done.39 = bf16[192,1728]{1,0:T(8,128)(2,1)S(1)} collective-permute-done((bf16[192,1728]{1,0:T(8,128)(2,1)S(1)}, bf16[192,1728]{1,0:T(8,128)(2,1)S(1)}, u32[]{:S(2)}, u32[]{:S(2)}) %collective-permute-start.39) | collective-permute-done | bytes 663584 | tf_op jit(solution)/shard_map/ppermute | solution.py:417
  (201 shorter events, 51.8 us)
Async XLA Ops:
  0.7 71.7 %collective-permute-start.4 = (bf16[192,768]{1,0:T(8,128)(2,1)}, bf16[192,768]{1,0:T(8,128)(2,1)}, u32[]{:S(2)}, u32[]{:S(2)}) collective-permute-start(bf16[192,768]{1,0:T(8,128)(2,1)} %param.14), channel_id=1, source_target_pairs={{0,1},{1,0},{2,3},{3,2},{4,5},{5,4},{6,7},{7,6},{8,9},{9,8},{10,11... | collective-permute-start | bytes 884744 | tf_op jit(solution)/shard_map/ppermute | solution.py:39
  1.2 27.6 %collective-permute-start.6 = (bf16[192,768]{1,0:T(8,128)(2,1)}, bf16[192,768]{1,0:T(8,128)(2,1)}, u32[]{:S(2)}, u32[]{:S(2)}) collective-permute-start(bf16[192,768]{1,0:T(8,128)(2,1)} %param.14), channel_id=1, source_target_pairs={{0,2},{1,3},{2,0},{3,1},{4,6},{5,7},{6,4},{7,5},{8,10},{9,11},{10,... | collective-permute-start | bytes 884744 | tf_op jit(solution)/shard_map/ppermute | solution.py:39
  7.9 20.6 %collective-permute-start.1 = (bf16[512,768]{1,0:T(8,128)(2,1)}, bf16[512,768]{1,0:T(8,128)(2,1)}, u32[]{:S(2)}, u32[]{:S(2)}) collective-permute-start(bf16[512,768]{1,0:T(8,128)(2,1)} %fusion.5), channel_id=1, source_target_pairs={{0,2},{1,3},{2,0},{3,1},{4,6},{5,7},{6,4},{7,5},{8,10},{9,11},{10,... | collective-permute-start | bytes 2359304 | tf_op jit(solution)/shard_map/ppermute | solution.py:39
  8.0 22.6 %collective-permute-start = (bf16[512,768]{1,0:T(8,128)(2,1)}, bf16[512,768]{1,0:T(8,128)(2,1)}, u32[]{:S(2)}, u32[]{:S(2)}) collective-permute-start(bf16[512,768]{1,0:T(8,128)(2,1)} %fusion.5), channel_id=1, source_target_pairs={{0,1},{1,0},{2,3},{3,2},{4,5},{5,4},{6,7},{7,6},{8,9},{9,8},{10,11... | collective-permute-start | bytes 2359304 | tf_op jit(solution)/shard_map/ppermute | solution.py:39
  8.1 95.5 %collective-permute-start.10 = (bf16[512,768]{1,0:T(8,128)(2,1)}, bf16[512,768]{1,0:T(8,128)(2,1)}, u32[]{:S(2)}, u32[]{:S(2)}) collective-permute-start(bf16[512,768]{1,0:T(8,128)(2,1)} %g_a_ref.1), channel_id=1, source_target_pairs={{0,1},{1,0},{2,3},{3,2},{4,5},{5,4},{6,7},{7,6},{8,9},{9,8},{10,11... | collective-permute-start | bytes 2359304 | tf_op jit(solution)/shard_map/ppermute | solution.py:39
  28.5 2.5 collective-permute-start.2
  28.8 56.8 %collective-permute-start.14 = (bf16[512,768]{1,0:T(8,128)(2,1)}, bf16[512,768]{1,0:T(8,128)(2,1)}, u32[]{:S(2)}, u32[]{:S(2)}) collective-permute-start(bf16[512,768]{1,0:T(8,128)(2,1)} %g_a_ref.1), channel_id=1, source_target_pairs={{0,2},{1,3},{2,0},{3,1},{4,6},{5,7},{6,4},{7,5},{8,10},{9,11},{10,... | collective-permute-start | bytes 2359304 | tf_op jit(solution)/shard_map/ppermute | solution.py:39
  30.6 45.0 %collective-permute-start.8 = (bf16[192,768]{1,0:T(8,128)(2,1)}, bf16[192,768]{1,0:T(8,128)(2,1)S(1)}, u32[]{:S(2)}, u32[]{:S(2)}) collective-permute-start(bf16[192,768]{1,0:T(8,128)(2,1)} %collective-permute-done.6), channel_id=1, source_target_pairs={{0,1},{1,0},{2,3},{3,2},{4,5},{5,4},{6,7},{7,6},{8,9},{9,8},{10,11... | collective-permute-start | bytes 884744 | tf_op jit(solution)/shard_map/ppermute | solution.py:39
  62.5 8.4 %collective-permute-start.5 = (bf16[512,192]{1,0:T(8,128)(2,1)S(1)}, bf16[512,192]{1,0:T(8,128)(2,1)S(1)}, u32[]{:S(2)}, u32[]{:S(2)}) collective-permute-start(bf16[512,192]{1,0:T(8,128)(2,1)S(1)} %get-tuple-element.94), channel_id=1, source_target_pairs={{0,2},{1,3},{2,0},{3,1},{4,6},{5,7},{6,4},{7,5},{8,10},{9,11},{10,... | collective-permute-start | bytes 589832 | tf_op jit(solution)/shard_map/ppermute | solution.py:39
  70.9 3.3 collective-permute-start.3
  72.3 8.2 %collective-permute-start.7 = (bf16[512,192]{1,0:T(8,128)(2,1)S(1)}, bf16[512,192]{1,0:T(8,128)(2,1)S(1)}, u32[]{:S(2)}, u32[]{:S(2)}) collective-permute-start(bf16[512,192]{1,0:T(8,128)(2,1)S(1)} %get-tuple-element.93), channel_id=1, source_target_pairs={{0,3},{1,2},{2,1},{3,0},{4,7},{5,6},{6,5},{7,4},{8,11},{9,10},{10,... | collective-permute-start | bytes 589832 | tf_op jit(solution)/shard_map/ppermute | solution.py:39
  82.3 21.3 %copy-start.9 = (bf16[512,768]{1,0:T(8,128)(2,1)}, bf16[512,768]{1,0:T(8,128)(2,1)S(1)}, u32[]{:S(2)}) copy-start(bf16[512,768]{1,0:T(8,128)(2,1)S(1)} %multiply_convert_fusion.x_a_ref) | copy-start | bytes 2359300
  82.3 21.3 %collective-permute-start.9 = (bf16[512,768]{1,0:T(8,128)(2,1)S(1)}, bf16[512,768]{1,0:T(8,128)(2,1)}, u32[]{:S(2)}, u32[]{:S(2)}) collective-permute-start(bf16[512,768]{1,0:T(8,128)(2,1)S(1)} %multiply_convert_fusion.x_a_ref), channel_id=1, source_target_pairs={{0,1},{1,0},{2,3},{3,2},{4,5},{5,4},{6,7},{7,6},{8,9},{9,8},{10,11... | collective-permute-start | bytes 2359304 | tf_op jit(solution)/shard_map/ppermute | solution.py:39
  83.6 12.3 %collective-permute-start.12 = (bf16[256,768]{1,0:T(8,128)(2,1)}, bf16[256,768]{1,0:T(8,128)(2,1)}, u32[]{:S(2)}, u32[]{:S(2)}) collective-permute-start(bf16[256,768]{1,0:T(8,128)(2,1)} %get-tuple-element.96), channel_id=1, source_target_pairs={{0,2},{1,3},{2,0},{3,1},{4,6},{5,7},{6,4},{7,5},{8,10},{9,11},{10,... | collective-permute-start | bytes 1179656 | tf_op jit(solution)/shard_map/ppermute | solution.py:39
  85.3 18.2 %collective-permute-start.16 = (bf16[256,768]{1,0:T(8,128)(2,1)}, bf16[256,768]{1,0:T(8,128)(2,1)}, u32[]{:S(2)}, u32[]{:S(2)}) collective-permute-start(bf16[256,768]{1,0:T(8,128)(2,1)} %get-tuple-element.97), channel_id=1, source_target_pairs={{0,2},{1,3},{2,0},{3,1},{4,6},{5,7},{6,4},{7,5},{8,10},{9,11},{10,... | collective-permute-start | bytes 1179656 | tf_op jit(solution)/shard_map/ppermute | solution.py:39
  85.6 32.1 %collective-permute-start.15 = (bf16[512,768]{1,0:T(8,128)(2,1)}, bf16[512,768]{1,0:T(8,128)(2,1)}, u32[]{:S(2)}, u32[]{:S(2)}) collective-permute-start(bf16[512,768]{1,0:T(8,128)(2,1)} %collective-permute-done.14.g_a_ref), channel_id=1, source_target_pairs={{0,1},{1,0},{2,3},{3,2},{4,5},{5,4},{6,7},{7,6},{8,9},{9,8},{10,11... | collective-permute-start | bytes 2359304 | tf_op jit(solution)/shard_map/ppermute | solution.py:39
  95.9 21.8 %collective-permute-start.13 = (bf16[256,768]{1,0:T(8,128)(2,1)}, bf16[256,768]{1,0:T(8,128)(2,1)S(1)}, u32[]{:S(2)}, u32[]{:S(2)}) collective-permute-start(bf16[256,768]{1,0:T(8,128)(2,1)} %collective-permute-done.12.x_a_ref), channel_id=1, source_target_pairs={{0,1},{1,0},{2,3},{3,2},{4,5},{5,4},{6,7},{7,6},{8,9},{9,8},{10,11... | collective-permute-start | bytes 1179656 | tf_op jit(solution)/shard_map/ppermute | solution.py:39
  103.6 26.6 %collective-permute-start.17 = (bf16[256,768]{1,0:T(8,128)(2,1)}, bf16[256,768]{1,0:T(8,128)(2,1)S(1)}, u32[]{:S(2)}, u32[]{:S(2)}) collective-permute-start(bf16[256,768]{1,0:T(8,128)(2,1)} %collective-permute-done.16.x_a_ref), channel_id=1, source_target_pairs={{0,1},{1,0},{2,3},{3,2},{4,5},{5,4},{6,7},{7,6},{8,9},{9,8},{10,11... | collective-permute-start | bytes 1179656 | tf_op jit(solution)/shard_map/ppermute | solution.py:39
  117.1 49.7 %collective-permute-start.11 = (bf16[512,768]{1,0:T(8,128)(2,1)}, bf16[512,768]{1,0:T(8,128)(2,1)S(1)}, u32[]{:S(2)}, u32[]{:S(2)}) collective-permute-start(bf16[512,768]{1,0:T(8,128)(2,1)} %get-tuple-element.30), channel_id=1, source_target_pairs={{0,1},{1,0},{2,3},{3,2},{4,5},{5,4},{6,7},{7,6},{8,9},{9,8},{10,11... | collective-permute-start | bytes 2359304 | tf_op jit(solution)/shard_map/ppermute | solution.py:39
  117.6 36.6 %collective-permute-start.20 = (bf16[512,768]{1,0:T(8,128)(2,1)}, bf16[512,768]{1,0:T(8,128)(2,1)S(1)}, u32[]{:S(2)}, u32[]{:S(2)}) collective-permute-start(bf16[512,768]{1,0:T(8,128)(2,1)} %get-tuple-element.40), channel_id=1, source_target_pairs={{0,1},{1,0},{2,3},{3,2},{4,5},{5,4},{6,7},{7,6},{8,9},{9,8},{10,11... | collective-permute-start | bytes 2359304 | tf_op jit(solution)/shard_map/ppermute | solution.py:39
  129.6 15.8 %collective-permute-start.21 = (bf16[256,768]{1,0:T(8,128)(2,1)}, bf16[256,768]{1,0:T(8,128)(2,1)S(1)}, u32[]{:S(2)}, u32[]{:S(2)}) collective-permute-start(bf16[256,768]{1,0:T(8,128)(2,1)} %get-tuple-element.42), channel_id=1, source_target_pairs={{0,1},{1,0},{2,3},{3,2},{4,5},{5,4},{6,7},{7,6},{8,9},{9,8},{10,11... | collective-permute-start | bytes 1179656 | tf_op jit(solution)/shard_map/ppermute | solution.py:39
  141.7 5.7 %collective-permute-start.23 = (bf16[256,768]{1,0:T(8,128)(2,1)}, bf16[256,768]{1,0:T(8,128)(2,1)S(1)}, u32[]{:S(2)}, u32[]{:S(2)}) collective-permute-start(bf16[256,768]{1,0:T(8,128)(2,1)} %get-tuple-element.44), channel_id=1, source_target_pairs={{0,1},{1,0},{2,3},{3,2},{4,5},{5,4},{6,7},{7,6},{8,9},{9,8},{10,11... | collective-permute-start | bytes 1179656 | tf_op jit(solution)/shard_map/ppermute | solution.py:39
  142.9 7.0 %collective-permute-start.18 = (bf16[512,768]{1,0:T(8,128)(2,1)S(1)}, bf16[512,768]{1,0:T(8,128)(2,1)S(1)}, u32[]{:S(2)}, u32[]{:S(2)}) collective-permute-start(bf16[512,768]{1,0:T(8,128)(2,1)S(1)} %pad_maximum_fusion.3), channel_id=1, source_target_pairs={{0,1},{1,0},{2,3},{3,2},{4,5},{5,4},{6,7},{7,6},{8,9},{9,8},{10,11... | collective-permute-start | bytes 2359304 | tf_op jit(solution)/shard_map/ppermute | solution.py:39
  145.5 12.0 %collective-permute-start.22 = (bf16[256,768]{1,0:T(8,128)(2,1)S(1)}, bf16[256,768]{1,0:T(8,128)(2,1)S(1)}, u32[]{:S(2)}, u32[]{:S(2)}) collective-permute-start(bf16[256,768]{1,0:T(8,128)(2,1)S(1)} %add_convert_fusion.4), channel_id=1, source_target_pairs={{0,2},{1,3},{2,0},{3,1},{4,6},{5,7},{6,4},{7,5},{8,10},{9,11},{10,... | collective-permute-start | bytes 1179656 | tf_op jit(solution)/shard_map/ppermute | solution.py:39
  147.5 18.5 %collective-permute-start.24 = (bf16[256,768]{1,0:T(8,128)(2,1)S(1)}, bf16[256,768]{1,0:T(8,128)(2,1)S(1)}, u32[]{:S(2)}, u32[]{:S(2)}) collective-permute-start(bf16[256,768]{1,0:T(8,128)(2,1)S(1)} %add_convert_fusion.3), channel_id=1, source_target_pairs={{0,2},{1,3},{2,0},{3,1},{4,6},{5,7},{6,4},{7,5},{8,10},{9,11},{10,... | collective-permute-start | bytes 1179656 | tf_op jit(solution)/shard_map/ppermute | solution.py:39
  150.0 16.0 %copy-start.3 = (f32[512,768]{1,0:T(8,128)S(1)}, f32[512,768]{1,0:T(8,128)}, u32[]{:S(2)}) copy-start(f32[512,768]{1,0:T(8,128)} %copy-done.2) | copy-start | bytes 4718596
  150.0 16.0 %copy-start.10 = (bf16[512,768]{1,0:T(8,128)(2,1)S(1)}, bf16[512,768]{1,0:T(8,128)(2,1)}, u32[]{:S(2)}) copy-start(bf16[512,768]{1,0:T(8,128)(2,1)} %get-tuple-element.39) | copy-start | bytes 2359300
  150.2 31.9 %collective-permute-start.19 = (bf16[512,768]{1,0:T(8,128)(2,1)S(1)}, bf16[512,768]{1,0:T(8,128)(2,1)S(1)}, u32[]{:S(2)}, u32[]{:S(2)}) collective-permute-start(bf16[512,768]{1,0:T(8,128)(2,1)S(1)} %add_convert_fusion.2), channel_id=1, source_target_pairs={{0,2},{1,3},{2,0},{3,1},{4,6},{5,7},{6,4},{7,5},{8,10},{9,11},{10,... | collective-permute-start | bytes 2359304 | tf_op jit(solution)/shard_map/ppermute | solution.py:39
  166.0 16.1 %copy-start.21 = (bf16[512,768]{1,0:T(8,128)(2,1)S(1)}, bf16[512,768]{1,0:T(8,128)(2,1)}, u32[]{:S(2)}) copy-start(bf16[512,768]{1,0:T(8,128)(2,1)} %get-tuple-element.29) | copy-start | bytes 2359300
  195.2 8.6 %collective-permute-start.27 = (bf16[512,192]{1,0:T(8,128)(2,1)}, bf16[512,192]{1,0:T(8,128)(2,1)S(1)}, u32[]{:S(2)}, u32[]{:S(2)}) collective-permute-start(bf16[512,192]{1,0:T(8,128)(2,1)} %copy.66), channel_id=1, source_target_pairs={{0,3},{1,2},{2,1},{3,0},{4,7},{5,6},{6,5},{7,4},{8,11},{9,10},{10,... | collective-permute-start | bytes 589832 | tf_op jit(solution)/shard_map/ppermute | solution.py:39
  195.9 13.8 %collective-permute-start.26 = (bf16[512,192]{1,0:T(8,128)(2,1)}, bf16[512,192]{1,0:T(8,128)(2,1)S(1)}, u32[]{:S(2)}, u32[]{:S(2)}) collective-permute-start(bf16[512,192]{1,0:T(8,128)(2,1)} %copy.65), channel_id=1, source_target_pairs={{0,2},{1,3},{2,0},{3,1},{4,6},{5,7},{6,4},{7,5},{8,10},{9,11},{10,... | collective-permute-start | bytes 589832 | tf_op jit(solution)/shard_map/ppermute | solution.py:39
  197.1 12.6 %collective-permute-start.25 = (bf16[512,192]{1,0:T(8,128)(2,1)}, bf16[512,192]{1,0:T(8,128)(2,1)S(1)}, u32[]{:S(2)}, u32[]{:S(2)}) collective-permute-start(bf16[512,192]{1,0:T(8,128)(2,1)} %copy.64), channel_id=1, source_target_pairs={{0,1},{1,0},{2,3},{3,2},{4,5},{5,4},{6,7},{7,6},{8,9},{9,8},{10,11... | collective-permute-start | bytes 589832 | tf_op jit(solution)/shard_map/ppermute | solution.py:39
  199.2 59.4 %collective-permute-start.34 = (bf16[768,192]{0,1:T(8,128)(2,1)}, bf16[768,192]{0,1:T(8,128)(2,1)}, u32[]{:S(2)}, u32[]{:S(2)}) collective-permute-start(bf16[768,192]{0,1:T(8,128)(2,1)} %convolution_convert_fusion.7), channel_id=1, source_target_pairs={{0,1},{1,0},{2,3},{3,2},{4,5},{5,4},{6,7},{7,6},{8,9},{9,8},{10,11... | collective-permute-start | bytes 884744 | tf_op jit(solution)/shard_map/ppermute | solution.py:39
  200.0 48.9 %collective-permute-start.35 = (bf16[768,192]{0,1:T(8,128)(2,1)S(1)}, bf16[768,192]{0,1:T(8,128)(2,1)S(1)}, u32[]{:S(2)}, u32[]{:S(2)}) collective-permute-start(bf16[768,192]{0,1:T(8,128)(2,1)S(1)} %convolution_convert_fusion.5), channel_id=1, source_target_pairs={{0,1},{1,0},{2,3},{3,2},{4,5},{5,4},{6,7},{7,6},{8,9},{9,8},{10,11... | collective-permute-start | bytes 884744 | tf_op jit(solution)/shard_map/ppermute | solution.py:39
  209.9 33.1 %copy-start.19 = (bf16[768,576]{0,1:T(8,128)(2,1)S(1)}, bf16[768,576]{0,1:T(8,128)(2,1)}, u32[]{:S(2)}) copy-start(bf16[768,576]{0,1:T(8,128)(2,1)} %param.13) | copy-start | bytes 2654212
  209.9 33.1 %copy-start.31 = (bf16[512,768]{1,0:T(8,128)(2,1)S(1)}, bf16[512,768]{1,0:T(8,128)(2,1)}, u32[]{:S(2)}) copy-start(bf16[512,768]{1,0:T(8,128)(2,1)} %copy-done.30) | copy-start | bytes 2359300
  249.3 9.3 %collective-permute-start.36 = (bf16[768,192]{0,1:T(8,128)(2,1)S(1)}, bf16[768,192]{0,1:T(8,128)(2,1)S(1)}, u32[]{:S(2)}, u32[]{:S(2)}) collective-permute-start(bf16[768,192]{0,1:T(8,128)(2,1)S(1)} %fusion.13), channel_id=1, source_target_pairs={{0,2},{1,3},{2,0},{3,1},{4,6},{5,7},{6,4},{7,5},{8,10},{9,11},{10,... | collective-permute-start | bytes 884744 | tf_op jit(solution)/shard_map/ppermute | solution.py:39
  251.9 98.7 %collective-permute-start.28 = (bf16[512,768]{1,0:T(8,128)(2,1)}, bf16[512,768]{1,0:T(8,128)(2,1)}, u32[]{:S(2)}, u32[]{:S(2)}) collective-permute-start(bf16[512,768]{1,0:T(8,128)(2,1)} %convolution_convert_fusion.3), channel_id=1, source_target_pairs={{0,1},{1,0},{2,3},{3,2},{4,5},{5,4},{6,7},{7,6},{8,9},{9,8},{10,11... | collective-permute-start | bytes 2359304 | tf_op jit(solution)/shard_map/ppermute | solution.py:39
  256.9 14.3 %collective-permute-start.31 = (bf16[2,192,576]{2,1,0:T(8,128)(2,1)}, bf16[2,192,576]{2,1,0:T(8,128)(2,1)}, u32[]{:S(2)}, u32[]{:S(2)}) collective-permute-start(bf16[2,192,576]{2,1,0:T(8,128)(2,1)} %fusion.25), channel_id=1, source_target_pairs={{0,4},{4,0},{8,12},{12,8},{1,5},{5,1},{9,13},{13,9},{2,6},{6,2},{1... | collective-permute-start | bytes 1327112 | tf_op jit(solution)/shard_map/ppermute | solution.py:39
  266.3 78.4 %collective-permute-start.37 = (bf16[2,192,1728]{2,1,0:T(8,128)(2,1)}, bf16[2,192,1728]{2,1,0:T(8,128)(2,1)}, u32[]{:S(2)}, u32[]{:S(2)}) collective-permute-start(bf16[2,192,1728]{2,1,0:T(8,128)(2,1)} %pad_maximum_fusion.1), channel_id=1, source_target_pairs={{0,4},{4,0},{8,12},{12,8},{1,5},{5,1},{9,13},{13,9},{2,6},{6,2},{1... | collective-permute-start | bytes 3981320 | tf_op jit(solution)/shard_map/ppermute | solution.py:39
  270.7 71.1 %collective-permute-start.29 = (bf16[512,768]{1,0:T(8,128)(2,1)}, bf16[512,768]{1,0:T(8,128)(2,1)}, u32[]{:S(2)}, u32[]{:S(2)}) collective-permute-start(bf16[512,768]{1,0:T(8,128)(2,1)} %convolution_convert_fusion.1), channel_id=1, source_target_pairs={{0,1},{1,0},{2,3},{3,2},{4,5},{5,4},{6,7},{7,6},{8,9},{9,8},{10,11... | collective-permute-start | bytes 2359304 | tf_op jit(solution)/shard_map/ppermute | solution.py:39
  275.1 63.1 %collective-permute-start.32 = (bf16[1,192,576]{2,1,0:T(8,128)(2,1)}, bf16[1,192,576]{2,1,0:T(8,128)(2,1)}, u32[]{:S(2)}, u32[]{:S(2)}) collective-permute-start(bf16[1,192,576]{2,1,0:T(8,128)(2,1)} %dynamic-slice_convert_fusion.3), channel_id=1, source_target_pairs={{0,8},{4,12},{8,0},{12,4},{1,9},{5,13},{9,1},{13,5},{2,10},{6,14},... | collective-permute-start | bytes 663560 | tf_op jit(solution)/shard_map/ppermute | solution.py:39
  339.4 10.3 %collective-permute-start.33 = (bf16[192,576]{1,0:T(8,128)(2,1)S(1)}, bf16[192,576]{1,0:T(8,128)(2,1)S(1)}, u32[]{:S(2)}, u32[]{:S(2)}) collective-permute-start(bf16[192,576]{1,0:T(8,128)(2,1)S(1)} %fusion.28), channel_id=1, source_target_pairs={{0,16},{16,0},{1,17},{17,1},{2,18},{18,2},{3,19},{19,3},{4,20},{20... | collective-permute-start | bytes 663560 | tf_op jit(solution)/shard_map/ppermute | solution.py:417
  344.0 17.5 %collective-permute-start.30 = (bf16[512,768]{1,0:T(8,128)(2,1)S(1)}, bf16[512,768]{1,0:T(8,128)(2,1)S(1)}, u32[]{:S(2)}, u32[]{:S(2)}) collective-permute-start(bf16[512,768]{1,0:T(8,128)(2,1)S(1)} %add_convert_fusion), channel_id=1, source_target_pairs={{0,2},{1,3},{2,0},{3,1},{4,6},{5,7},{6,4},{7,5},{8,10},{9,11},{10,... | collective-permute-start | bytes 2359304 | tf_op jit(solution)/shard_map/ppermute | solution.py:39
  347.7 13.7 %copy-start.5 = (bf16[512,768]{1,0:T(8,128)(2,1)S(1)}, bf16[512,768]{1,0:T(8,128)(2,1)}, u32[]{:S(2)}) copy-start(bf16[512,768]{1,0:T(8,128)(2,1)} %param.10) | copy-start | bytes 2359300
  347.8 31.3 %collective-permute-start.38 = (bf16[1,192,1728]{2,1,0:T(8,128)(2,1)S(1)}, bf16[1,192,1728]{2,1,0:T(8,128)(2,1)S(1)}, u32[]{:S(2)}, u32[]{:S(2)}) collective-permute-start(bf16[1,192,1728]{2,1,0:T(8,128)(2,1)S(1)} %pad_maximum_fusion.4), channel_id=1, source_target_pairs={{0,8},{4,12},{8,0},{12,4},{1,9},{5,13},{9,1},{13,5},{2,10},{6,14},... | collective-permute-start | bytes 1990664 | tf_op jit(solution)/shard_map/ppermute | solution.py:39
  363.8 16.5 %copy-start.7 = (f32[512,768]{1,0:T(8,128)S(1)}, f32[512,768]{1,0:T(8,128)}, u32[]{:S(2)}) copy-start(f32[512,768]{1,0:T(8,128)} %get-tuple-element.87) | copy-start | bytes 4718596
  379.4 17.4 %collective-permute-start.39 = (bf16[192,1728]{1,0:T(8,128)(2,1)S(1)}, bf16[192,1728]{1,0:T(8,128)(2,1)S(1)}, u32[]{:S(2)}, u32[]{:S(2)}) collective-permute-start(bf16[192,1728]{1,0:T(8,128)(2,1)S(1)} %pad_maximum_fusion.5), channel_id=1, source_target_pairs={{0,16},{16,0},{1,17},{17,1},{2,18},{18,2},{3,19},{19,3},{4,20},{20... | collective-permute-start | bytes 1990664 | tf_op jit(solution)/shard_map/ppermute | solution.py:417
  (26 other events, 115.5 us)
